TPU v7x, 32 devices: a whole 2x2x4 slice. The times are simulated.
32 devices in a mesh: req: 16 (over z, y, x), tp: 2 (over core).
Axes of the slice: x: 2, y: 2, z: 4, core: 2. Of those that a mesh axis runs over, the one named last changes fastest.
Arguments:
- queries: bfloat16 [4096, 2048], P('req', 'tp'), may hold values from -10 to 10
- new_kv: bfloat16 [4096, 2048], P('req', 'tp'), may hold values from -4 to 4
- kv_pool: bfloat16 [128, 4, 256, 2048], P('req', None, None, 'tp'), may hold values from -4 to 4
- cache_lens: int32 [128], P('req'), may hold values from 2 to 1024, as said below
- parents: int32 [128, 32], P('req'), may hold values from 0 to 31, as said below
- accepted: int32 [128], P('req'), may hold values from 0 to 31, as said below
- residual: bfloat16 [4096, 4096], P(('req', 'tp')), may hold values from -3 to 3
- w_out: bfloat16 [2048, 4096], P('tp'), may hold values from -0.125 to 0.125
- norm_gain: float32 [4096], replicated, may hold values from 0.25 to 1.75
Outputs:
- hidden_out: bfloat16 [4096, 4096], P(('req', 'tp'))
- normed: bfloat16 [4096, 4096], P(('req', 'tp'))
- accepted_kv: bfloat16 [128, 8, 2048], P('req', None, 'tp')
Inputs may be any that keep to these rules, and one draw needn't show every extreme that they name: parents[r, 0] = 0 and parents[r, i] < i for i >= 1; every node lies at depth 7 or less; nodes 1 to 7 form a chain below the root. Some request's accepted node lies at depth 7. `cache_lens`: some request holds 1024 cached rows and some holds 2.
All inputs are finite; a program needn't handle non-finite values.
Results may differ from a plain program's by a relative error of at most 0.015.
Values may be sent and summed in bfloat16 or wider, within the bound.
A program may use at most 128 MiB of HBM per device.

v0:
```python
from functools import reduce

import jax
import jax.numpy as jnp
from jax import lax
from jax.sharding import PartitionSpec as P

HD = 128
TREE = 32
MAXD = 7
PATH = 8


NEGATIVE = -1e30


def shifted(value, axis, steps):
    count = lax.axis_size(axis)
    pairs = [(source, (source + steps) % count) for source in range(count)]
    return lax.ppermute(value, axis, pairs)


def ancestors(parents):
    node_ids = jnp.arange(TREE, dtype=jnp.int32)
    current = jnp.broadcast_to(node_ids, parents.shape)
    marked = jnp.zeros(parents.shape + (TREE,), jnp.int32)
    for depth_step in range(MAXD + 1):
        onehot_rows = (current[..., None] == node_ids).astype(jnp.int32)
        marked = jnp.maximum(marked, onehot_rows)
        current = jnp.sum(onehot_rows * parents[..., None, :], axis=-1, dtype=jnp.int32)
    return marked


def block_partial(query_rows, key_rows, value_rows, allowed):
    scale_factor = HD ** (-0.5)
    scores = (
        jnp.einsum("rtkgd,rckd->rtkgc", query_rows, key_rows, preferred_element_type=jnp.float32)
        * scale_factor
    )
    visible = allowed[:, :, None, None, :]
    largest = jnp.max(jnp.where(visible, scores, NEGATIVE), axis=-1)
    weights = jnp.where(visible, jnp.exp(scores - largest[..., None]), 0.0)
    totals = jnp.sum(weights, axis=-1)
    weighted = jnp.einsum(
        "rtkgc,rckd->rtkgd",
        weights.astype(jnp.bfloat16),
        value_rows,
        preferred_element_type=jnp.float32,
    )
    return (largest, totals, weighted)


def page_term(query_rows, page_rows, lengths, page_index):
    req_count, row_count, row_width = page_rows.shape
    kv_local = row_width // (2 * HD)
    split_rows = page_rows.reshape(req_count, row_count, kv_local, 2, HD)
    positions = page_index * row_count + jnp.arange(row_count, dtype=jnp.int32)
    allowed = positions[None, None, :] < lengths[:, None, None]
    return block_partial(query_rows, split_rows[:, :, :, 0], split_rows[:, :, :, 1], allowed)


def merge_blocks(block_list):
    largest = reduce(jnp.maximum, [block_part[0] for block_part in block_list])
    factors = [jnp.exp(block_part[0] - largest) for block_part in block_list]
    denominator = reduce(
        jnp.add, [factor * block_part[1] for factor, block_part in zip(factors, block_list)]
    )
    numerator = reduce(
        jnp.add,
        [factor[..., None] * block_part[2] for factor, block_part in zip(factors, block_list)],
    )
    return (denominator, numerator)


def per_device(queries, new_kv, kv_pool, cache_lens, parents, accepted, residual, w_out, norm_gain):
    req_count, page_count, page_size, row_width = kv_pool.shape
    kv_local = row_width // (2 * HD)
    q_local = queries.shape[1] // HD
    group = q_local // kv_local
    query_rows = queries.reshape(req_count, TREE, kv_local, group, HD)
    fresh = new_kv.reshape(req_count, TREE, kv_local, 2, HD)
    marked = ancestors(parents)
    block_list = [block_partial(query_rows, fresh[:, :, :, 0], fresh[:, :, :, 1], marked > 0)]
    for page_index in range(page_count):
        page_rows = kv_pool[:, page_index]
        if page_index > 0:
            page_rows = shifted(page_rows, "req", -page_index)
        block_list.append(page_term(query_rows, page_rows, cache_lens, page_index))
    denominator, numerator = merge_blocks(block_list)
    attention = (
        (numerator / denominator[..., None])
        .astype(jnp.bfloat16)
        .reshape(req_count * TREE, q_local * HD)
    )
    product = jnp.dot(attention, w_out, preferred_element_type=jnp.float32)
    summed = lax.psum_scatter(
        lax.optimization_barrier(product.astype(jnp.bfloat16))
        .astype(jnp.float32)
        .astype(jnp.bfloat16),
        "tp",
        scatter_dimension=0,
        tiled=True,
    ).astype(jnp.float32)
    hidden_out = (residual.astype(jnp.float32) + summed).astype(jnp.bfloat16)
    widened = hidden_out.astype(jnp.float32)
    normed = (
        widened * lax.rsqrt(jnp.mean(widened * widened, axis=-1, keepdims=True) + 1e-05) * norm_gain
    ).astype(jnp.bfloat16)
    node_ids = jnp.arange(TREE, dtype=jnp.int32)
    chosen = (accepted[:, None] == node_ids[None, :]).astype(jnp.int32)
    on_path = jnp.sum(chosen[:, :, None] * marked, axis=1, dtype=jnp.int32)
    path_rank = jnp.cumsum(on_path, axis=1, dtype=jnp.int32) - 1
    path_slots = jnp.arange(PATH, dtype=jnp.int32)
    selector = (
        (path_rank[:, None, :] == path_slots[None, :, None]) & (on_path[:, None, :] > 0)
    ).astype(jnp.bfloat16)
    fresh_rows = new_kv.reshape(req_count, TREE, row_width)
    accepted_kv = jnp.einsum(
        "rku,ruc->rkc", selector, fresh_rows, preferred_element_type=jnp.float32
    ).astype(jnp.bfloat16)
    return (hidden_out, normed, accepted_kv)


def solution(mesh):
    placed = (
        P("req", "tp"),
        P("req", "tp"),
        P("req", None, None, "tp"),
        P("req"),
        P("req", None),
        P("req"),
        P(("req", "tp"), None),
        P("tp", None),
        P(),
    )
    return jax.shard_map(
        per_device,
        mesh=mesh,
        in_specs=placed,
        out_specs=(P(("req", "tp"), None), P(("req", "tp"), None), P("req", None, "tp")),
        check_vma=False,
    )
```

profile of v0, /device:TPU:0, one launch (start us, length us, event | category | flops | bytes accessed | tf_op | source)
XLA Modules:
  0.0 347.3 jit_solution(8318307905658818010)
XLA Ops:
  7.2 12.2 %fusion.93 = (bf16[8,1,256,1024]{3,2,1,0:T(8,128)(2,1)}, bf16[8,1,256,1024]{3,2,1,0:T(8,128)(2,1)}, bf16[8,1,256,1024]{3,2,1,0:T(8,128)(2,1)}, bf16[8,1,256,1024]{3,2,1,0:T(8,128)(2,1)}) fusion(bf16[8,4,256,1024]{3,2,1,0:T(8,128)(2,1)} %param.11), kind=kLoop, calls=%fused_computation.150 | loop fusion | bytes 33554432 | tf_op jit(solution)/shard_map/slice | solution.py:85
  19.4 6.5 %copy.57 = bf16[8,1,256,1024]{2,3,0,1:T(8,128)(2,1)} copy(bf16[8,1,256,1024]{3,2,1,0:T(8,128)(2,1)} %get-tuple-element.14) | data formatting | bytes 8388608
  25.9 6.0 %collective-permute-start.2 = (bf16[8,256,1024]{1,2,0:T(8,128)(2,1)}, bf16[8,256,1024]{1,2,0:T(8,128)(2,1)}, u32[]{:S(2)}, u32[]{:S(2)}) collective-permute-start(bf16[8,256,1024]{1,2,0:T(8,128)(2,1)} %bitcast.225), channel_id=1, source_target_pairs={{0,26},{2,28},{4,30},{6,0},{8,2},{10,4},{12,6},{14,8},{16,10},{18,... | collective-permute-start | bytes 12582920 | tf_op jit(solution)/shard_map/ppermute | solution.py:20
  31.8 6.4 %copy.55 = bf16[8,1,256,1024]{2,3,0,1:T(8,128)(2,1)} copy(bf16[8,1,256,1024]{3,2,1,0:T(8,128)(2,1)} %get-tuple-element.12) | data formatting | bytes 8388608
  38.3 1.4 collective-permute-start.1
  39.7 6.5 %copy.53 = bf16[8,1,256,1024]{2,3,0,1:T(8,128)(2,1)} copy(bf16[8,1,256,1024]{3,2,1,0:T(8,128)(2,1)} %get-tuple-element.13) | data formatting | bytes 8388608
  46.2 1.4 collective-permute-start
  47.6 0.4 reshape.318
  48.0 6.5 %copy.51 = bf16[8,1,256,1024]{2,3,0,1:T(8,128)(2,1)} copy(bf16[8,1,256,1024]{3,2,1,0:T(8,128)(2,1)} %get-tuple-element.11) | data formatting | bytes 8388608
  54.5 0.4 reshape.317
  55.0 0.1 select_reduce_fusion.7
  55.1 0.1 select_reduce_fusion.6
  55.2 0.1 select_reduce_fusion.5
  55.3 0.1 select_reduce_fusion.4
  55.4 0.1 select_reduce_fusion.3
  55.5 0.1 select_reduce_fusion.2
  55.6 0.1 select_reduce_fusion.1
  55.8 0.2 fusion.78
  55.9 0.7 fusion.94
  56.7 0.9 select_reduce_fusion
  57.6 0.3 fusion.67
  58.0 0.1 iota_compare_fusion.9
  58.0 0.1 copy-done.1
  58.1 0.7 fusion.20
  58.8 64.3 %collective-permute-done.2 = bf16[8,256,1024]{1,2,0:T(8,128)(2,1)} collective-permute-done((bf16[8,256,1024]{1,2,0:T(8,128)(2,1)}, bf16[8,256,1024]{1,2,0:T(8,128)(2,1)}, u32[]{:S(2)}, u32[]{:S(2)}) %collective-permute-start.2) | collective-permute-done | bytes 4194336 | tf_op jit(solution)/shard_map/ppermute | solution.py:20
  123.1 2.2 fusion.11
  125.4 88.5 %collective-permute-done.1 = bf16[8,256,1024]{1,2,0:T(8,128)(2,1)} collective-permute-done((bf16[8,256,1024]{1,2,0:T(8,128)(2,1)}, bf16[8,256,1024]{1,2,0:T(8,128)(2,1)}, u32[]{:S(2)}, u32[]{:S(2)}) %collective-permute-start.1) | collective-permute-done | bytes 4194336 | tf_op jit(solution)/shard_map/ppermute | solution.py:20
  213.9 2.2 fusion.14
  216.1 86.5 %collective-permute-done = bf16[8,256,1024]{1,2,0:T(8,128)(2,1)} collective-permute-done((bf16[8,256,1024]{1,2,0:T(8,128)(2,1)}, bf16[8,256,1024]{1,2,0:T(8,128)(2,1)}, u32[]{:S(2)}, u32[]{:S(2)}) %collective-permute-start) | collective-permute-done | bytes 4194336 | tf_op jit(solution)/shard_map/ppermute | solution.py:20
  302.6 2.2 fusion.17
  304.8 1.5 fusion.27
  306.4 1.5 fusion.23
  308.0 2.4 fusion.38
  310.4 2.4 fusion.36
  312.7 1.6 fusion.32
  314.4 0.6 fusion.40
  314.9 2.8 fusion.46
  317.8 0.4 copy.38
  318.2 0.4 reshape.322
  318.6 7.1 %convolution_convert_fusion = bf16[256,4096]{1,0:T(8,128)(2,1)} fusion(bf16[256,1024]{1,0:T(8,128)(2,1)S(1)} %reshape.322, bf16[1024,4096]{1,0:T(8,128)(2,1)} %param.16), kind=kOutput, calls=%fused_computation | convolution fusion | flops 2148532224 | bytes 11010048 | tf_op jit(solution)/shard_map/dot_general | solution.py:95
  325.7 0.6 copy-done.8
  326.3 0.1 fusion.83
  326.4 0.2 multiply_reduce_fusion
  326.6 0.2 reduce_window_sum.11
  326.8 0.8 convolution_convert_fusion.1
  327.7 9.7 %reduce-scatter.2.cloned.1.call-done = bf16[128,4096]{1,0:T(8,128)(2,1)} async-done(((bf16[256,4096]{1,0:T(8,128)(2,1)}), bf16[128,4096]{1,0:T(8,128)(2,1)}) %reduce-scatter.2.cloned.1.call-update) | async-done | bytes 1048592 | tf_op jit(solution)/shard_map/reduce_scatter | solution.py:96
  337.4 1.7 fusion
  339.1 1.3 fusion.2
  (25 shorter events, 0.2 us)
Async XLA Ops:
  7.2 330.3 %reduce-scatter.2.cloned.1.call-start = ((), (), s32[]{:S(2)}) async-start(), calls=%async_computation.1 | async-start | bytes 3145728 | tf_op jit(solution)/shard_map/reduce_scatter | solution.py:96
  25.9 97.3 %collective-permute-start.2 = (bf16[8,256,1024]{1,2,0:T(8,128)(2,1)}, bf16[8,256,1024]{1,2,0:T(8,128)(2,1)}, u32[]{:S(2)}, u32[]{:S(2)}) collective-permute-start(bf16[8,256,1024]{1,2,0:T(8,128)(2,1)} %bitcast.225), channel_id=1, source_target_pairs={{0,26},{2,28},{4,30},{6,0},{8,2},{10,4},{12,6},{14,8},{16,10},{18,... | collective-permute-start | bytes 12582920 | tf_op jit(solution)/shard_map/ppermute | solution.py:20
  38.3 175.6 %collective-permute-start.1 = (bf16[8,256,1024]{1,2,0:T(8,128)(2,1)}, bf16[8,256,1024]{1,2,0:T(8,128)(2,1)}, u32[]{:S(2)}, u32[]{:S(2)}) collective-permute-start(bf16[8,256,1024]{1,2,0:T(8,128)(2,1)} %bitcast.224), channel_id=1, source_target_pairs={{0,28},{2,30},{4,0},{6,2},{8,4},{10,6},{12,8},{14,10},{16,12},{18,... | collective-permute-start | bytes 12582920 | tf_op jit(solution)/shard_map/ppermute | solution.py:20
  39.7 8.0 %copy-start.4 = (bf16[256,1024]{1,0:T(8,128)(2,1)S(1)}, bf16[256,1024]{1,0:T(8,128)(2,1)}, u32[]{:S(2)}) copy-start(bf16[256,1024]{1,0:T(8,128)(2,1)} %param.9) | copy-start | bytes 1572868
  46.2 256.4 %collective-permute-start = (bf16[8,256,1024]{1,2,0:T(8,128)(2,1)}, bf16[8,256,1024]{1,2,0:T(8,128)(2,1)}, u32[]{:S(2)}, u32[]{:S(2)}) collective-permute-start(bf16[8,256,1024]{1,2,0:T(8,128)(2,1)} %bitcast.223), channel_id=1, source_target_pairs={{0,30},{2,0},{4,2},{6,4},{8,6},{10,8},{12,10},{14,12},{16,14},{18,... | collective-permute-start | bytes 12582920 | tf_op jit(solution)/shard_map/ppermute | solution.py:20
  48.0 6.5 %copy-start.2 = (bf16[256,1024]{1,0:T(8,128)(2,1)S(1)}, bf16[256,1024]{1,0:T(8,128)(2,1)}, u32[]{:S(2)}) copy-start(bf16[256,1024]{1,0:T(8,128)(2,1)} %param.10) | copy-start | bytes 1572868
  48.0 6.9 %copy-start.5 = (s32[8,32]{1,0:T(8,128)S(1)}, s32[8,32]{1,0:T(8,128)}, u32[]{:S(2)}) copy-start(s32[8,32]{1,0:T(8,128)} %param.13) | copy-start | bytes 3076
  55.9 2.0 copy-start.7
  55.9 2.2 copy-start.1
  325.7 0.7 copy-start.8
  325.7 11.8 %copy-start.3 = (bf16[128,4096]{1,0:T(8,128)(2,1)S(1)}, bf16[128,4096]{1,0:T(8,128)(2,1)}, u32[]{:S(2)}) copy-start(bf16[128,4096]{1,0:T(8,128)(2,1)} %param.15) | copy-start | bytes 3145732
  326.3 12.8 %copy-start.6 = (f32[4096]{0:T(1024)S(1)}, f32[4096]{0:T(1024)}, u32[]{:S(2)}) copy-start(f32[4096]{0:T(1024)} %param.17) | copy-start | bytes 49156
  339.1 1.4 copy-start
Sparse Core Ops, SparseCore 0:
  325.8 11.5 reduce-scatter.1
where the time goes:
time: 348 us; the launch traced here: 347 us
  waiting for transfers between devices  249 us (72%)
  local copies, waits for them, and re-layouts  41.1 us (12%)
  matrix products  26 us (7%)
  between operations  14.3 us (4%)
  starting transfers between devices  8.85 us (3%)
  other arithmetic  8 us (2%)
    ppermute x3, waiting for transfers between devices, shifted(): return lax.ppermute(value, axis, pairs)  239 us
    unnamed x22, local copies, waits for them, and re-layouts  26.7 us
    slice x1, local copies, waits for them, and re-layouts, per_device(): page_rows = kv_pool[:, page_index]  12.2 us
    dot_general x5, matrix products, block_partial(): jnp.einsum('rtkgc,rckd->rtkgd', weights.astype(jnp.bfloat16), value_rows,...  9.78 us
    reduce_scatter x1, waiting for transfers between devices, per_device(): lax.psum_scatter(lax.optimization_barrier(product.astype(jnp.bfloat16)).a...  9.74 us
    ppermute x3, starting transfers between devices, shifted(): return lax.ppermute(value, axis, pairs)  8.82 us
    dot_general x5, matrix products, block_partial(): jnp.einsum('rtkgd,rckd->rtkgc', query_rows, key_rows, preferred_element_t...  8.26 us
    dot_general x1, matrix products, per_device(): product = jnp.dot(attention, w_out, preferred_element_type=jnp.float32)  7.07 us
  transfers between devices with their start and end apart: 4, of which 4 were waited for; matrix products, arithmetic and copies ran while one was open for 9% of the time, Pallas kernels for 0%

commit v1 on v0

v1 whole, which is shorter than its diff:
```python
import functools

import jax
import jax.numpy as jnp
from jax import lax
from jax.experimental import pallas as pl
from jax.experimental.pallas import tpu as pltpu
from jax.sharding import PartitionSpec as P

HD = 128
TREE = 32
PATH = 8
LANES = 128
NEGATIVE = -1e30
FLOOR = -1e29
SCALE2 = HD**-0.5 * 1.4426950408889634
MESH = pl.DeviceIdType.MESH
F32 = jnp.float32
BF16 = jnp.bfloat16


def iota(shape, axis):
    return lax.broadcasted_iota(jnp.int32, shape, axis)


def dot(left, right):
    return jnp.dot(left, right, preferred_element_type=F32)


def dot_t(left, right):
    return lax.dot_general(left, right, (((1,), (1,)), ((), ())), preferred_element_type=F32)


def indicator(mask, dtype=BF16):
    return jnp.where(mask, 1.0, 0.0).astype(dtype)


def tree_masks(parents, tokens):
    requests = tokens // TREE
    expand = indicator((iota((tokens, requests), 0) >> 5) == iota((tokens, requests), 1), F32)
    spread = dot(expand, parents.astype(F32))
    pick = (iota((tokens, TREE), 0) & (TREE - 1)) == iota((tokens, TREE), 1)
    parent = jnp.sum(jnp.where(pick, spread, 0.0), axis=1, keepdims=True)
    rows, columns = iota((tokens, tokens), 0), iota((tokens, tokens), 1)
    base = (rows & ~(TREE - 1)).astype(F32)
    one = indicator(columns.astype(F32) == parent + base, F32)
    eye = indicator(rows == columns, F32)
    two = dot(one.astype(BF16), one.astype(BF16))
    four = dot(two.astype(BF16), two.astype(BF16))
    reach = dot((eye + one).astype(BF16), (eye + two).astype(BF16))
    reach = dot(reach.astype(BF16), (eye + four).astype(BF16))
    return indicator(reach > 0.0)


def kernel(
    n_req, n_tp, chunk,
    lens_s, accepted_s, parents_ref, q_ref, fresh_ref, kv_hbm, residual_hbm, w_hbm, gain_ref,
    hidden_ref, normed_ref, path_ref,
    kv, w, residual, q_in, lens_own, lens_in, out_send, out_in, lse_send, lse_in,
    local_out, local_lse, lse_tile, tree, attention, own, proj_send, proj_in,
    load_sem, lens_send_sem, lens_recv_sem, q_send_sem, q_recv_sem, o_send_sem, o_recv_sem,
    l_send_sem, l_recv_sem, p_send_sem, p_recv_sem,
):
    me, tp = lax.axis_index("req"), lax.axis_index("tp")
    tokens, width = q_ref.shape
    requests = tokens // TREE
    heads = width // HD
    kv_heads = fresh_ref.shape[1] // (2 * HD)
    pages, page = kv.shape[0], kv.shape[2]
    part = tokens // n_tp
    per_part = part // chunk
    chunks = tokens // chunk
    features = w.shape[1]
    group = heads // kv_heads

    loads = [
        pltpu.make_async_copy(kv_hbm.at[:, p], kv.at[p], load_sem.at[p]) for p in range(pages)
    ]
    loads.append(pltpu.make_async_copy(w_hbm, w, load_sem.at[pages]))
    loads.append(pltpu.make_async_copy(residual_hbm, residual, load_sem.at[pages + 1]))
    for load in loads:
        load.start()

    def ahead(p):
        return lax.rem(me + p, n_req)

    def behind(p):
        return lax.rem(me + n_req - p, n_req)

    barrier = pltpu.get_barrier_semaphore()
    for p in range(1, pages):
        for other in (ahead(p), behind(p)):
            pl.semaphore_signal(barrier, inc=1, device_id={"req": other}, device_id_type=MESH)
    for j in range(1, n_tp):
        pl.semaphore_signal(
            barrier, inc=1, device_id={"tp": lax.rem(tp + j, n_tp)}, device_id_type=MESH
        )

    lens = jnp.zeros((requests, LANES), jnp.int32)
    for r in range(requests):
        lens = jnp.where(iota((requests, LANES), 0) == r, lens_s[r], lens)
    lens_own[...] = lens
    pl.semaphore_wait(barrier, 2 * (pages - 1) + n_tp - 1)

    def first_row(c):
        block = lax.rem(tp + 1 + c // per_part, n_tp)
        return pl.multiple_of(block * part + lax.rem(c, per_part) * chunk, chunk)

    def send_lens(p):
        return pltpu.make_async_remote_copy(
            lens_own, lens_in.at[p - 1], lens_send_sem.at[p - 1], lens_recv_sem.at[p - 1],
            device_id={"req": ahead(p)}, device_id_type=MESH,
        )

    def send_q(p, c):
        rows = pl.ds(first_row(c), chunk)
        return pltpu.make_async_remote_copy(
            q_ref.at[rows], q_in.at[p - 1, rows], q_send_sem.at[p - 1, c], q_recv_sem.at[p - 1, c],
            device_id={"req": ahead(p)}, device_id_type=MESH,
        )

    def send_out(p, c):
        rows = pl.ds(first_row(c), chunk)
        return pltpu.make_async_remote_copy(
            out_send.at[p - 1, rows], out_in.at[p - 1, rows],
            o_send_sem.at[p - 1, c], o_recv_sem.at[p - 1, c],
            device_id={"req": behind(p)}, device_id_type=MESH,
        )

    def send_lse(p, c):
        return pltpu.make_async_remote_copy(
            lse_send.at[p - 1, c], lse_in.at[p - 1, c],
            l_send_sem.at[p - 1, c], l_recv_sem.at[p - 1, c],
            device_id={"req": behind(p)}, device_id_type=MESH,
        )

    def send_proj(j):
        return pltpu.make_async_remote_copy(
            proj_send.at[j], proj_in.at[j], p_send_sem.at[j], p_recv_sem.at[j],
            device_id={"tp": lax.rem(tp + 1 + j, n_tp)}, device_id_type=MESH,
        )

    for p in range(1, pages):
        send_lens(p).start()

    @pl.loop(0, chunks)
    def _(c):
        for p in range(1, pages):
            send_q(p, c).start()

    marked = tree_masks(parents_ref[...], tokens)
    fold = indicator((iota((tokens, TREE), 0) & (TREE - 1)) == iota((tokens, TREE), 1))
    tree[...] = dot(marked, fold)
    accepted = jnp.zeros((requests, tokens), jnp.int32)
    for r in range(requests):
        accepted = jnp.where(iota((requests, tokens), 0) == r, accepted_s[r] + r * TREE, accepted)
    chosen = indicator(iota((requests, tokens), 1) == accepted, F32)
    on_path = dot(chosen, marked.astype(F32))
    upto = indicator(iota((tokens, tokens), 0) <= iota((tokens, tokens), 1), F32)
    count = dot(on_path, upto)
    slots = (requests * PATH, requests)
    spread = indicator((iota(slots, 0) >> 3) == iota(slots, 1), F32)
    slot = (iota((requests * PATH, tokens), 0) & (PATH - 1)).astype(F32) + 1.0
    selector = (dot(spread, count) == slot) & (dot(spread, on_path) > 0.0)
    path_ref[...] = dot(indicator(selector), fresh_ref[...]).astype(BF16)

    lane = iota((TREE, LANES), 1)

    def stacked_queries(ref, rows, k):
        columns = [slice((k * group + g) * HD, (k * group + g + 1) * HD) for g in range(group)]
        return jnp.concatenate([ref[rows, c] for c in columns], axis=0)

    def lens_mask(row, p):
        wide = jnp.concatenate([row] * (page // LANES), axis=1)
        return iota((1, page), 1) + p * page < wide

    loads[0].wait()

    @pl.loop(0, requests)
    def _(r):
        rows = pl.ds(pl.multiple_of(r * TREE, TREE), TREE)
        valid = lens_mask(lens_own[pl.ds(r, 1), :], 0)
        allowed = jnp.concatenate([tree[rows, :]] * group, axis=0) > 0.0
        lse = jnp.zeros((TREE, LANES), F32)
        for k in range(kv_heads):
            keys = slice(2 * k * HD, (2 * k + 1) * HD)
            values = slice((2 * k + 1) * HD, (2 * k + 2) * HD)
            query = stacked_queries(q_ref, rows, k)
            cached = jnp.where(valid, dot_t(query, kv[0, r, :, keys]) * SCALE2, NEGATIVE)
            drafted = jnp.where(allowed, dot_t(query, fresh_ref[rows, keys]) * SCALE2, NEGATIVE)
            largest = jnp.maximum(
                jnp.max(cached, axis=1, keepdims=True), jnp.max(drafted, axis=1, keepdims=True)
            )
            cached = jnp.exp2(cached - largest)
            drafted = jnp.exp2(drafted - largest)
            total = jnp.sum(cached, axis=1, keepdims=True) + jnp.sum(drafted, axis=1, keepdims=True)
            out = dot(cached.astype(BF16), kv[0, r, :, values])
            out = out + dot(drafted.astype(BF16), fresh_ref[rows, values])
            out = out / total
            level = largest + jnp.log2(total)
            for g in range(group):
                h = k * group + g
                some = slice(g * TREE, (g + 1) * TREE)
                local_out[rows, h * HD : (h + 1) * HD] = out[some]
                lse = jnp.where(lane == h, level[some], lse)
        local_lse[rows, :] = lse

    for p in range(1, pages):
        loads[p].wait()
        send_lens(p).wait_recv()

    @pl.loop(0, chunks)
    def _(c):
        start = first_row(c)
        for p in range(1, pages):
            send_q(p, c).wait_recv()

            @pl.loop(0, chunk // TREE)
            def _(i):
                r = start // TREE + i
                rows = pl.ds(pl.multiple_of(start + i * TREE, TREE), TREE)
                valid = lens_mask(lens_in[p - 1, pl.ds(r, 1), :], p)
                lse = jnp.zeros((TREE, LANES), F32)
                for k in range(kv_heads):
                    keys = slice(2 * k * HD, (2 * k + 1) * HD)
                    values = slice((2 * k + 1) * HD, (2 * k + 2) * HD)
                    query = stacked_queries(q_in.at[p - 1], rows, k)
                    cached = jnp.where(valid, dot_t(query, kv[p, r, :, keys]) * SCALE2, NEGATIVE)
                    largest = jnp.max(cached, axis=1, keepdims=True)
                    cached = jnp.exp2(cached - jnp.maximum(largest, FLOOR))
                    total = jnp.sum(cached, axis=1, keepdims=True)
                    out = dot(cached.astype(BF16), kv[p, r, :, values])
                    some_valid = total > 0.0
                    safe = jnp.where(some_valid, total, 1.0)
                    out = out / safe
                    level = jnp.where(some_valid, largest + jnp.log2(safe), NEGATIVE)
                    for g in range(group):
                        h = k * group + g
                        some = slice(g * TREE, (g + 1) * TREE)
                        out_send[p - 1, rows, h * HD : (h + 1) * HD] = out[some].astype(BF16)
                        lse = jnp.where(lane == h, level[some], lse)
                lse_tile[pl.ds(pl.multiple_of(i * TREE, TREE), TREE), :] = lse

            lse_send[p - 1, c] = lse_tile[...].T[:8]
            send_lse(p, c).start()
            send_out(p, c).start()

    loads[pages].wait()
    loads[pages + 1].wait()

    for j in range(n_tp):

        @pl.loop(0, per_part)
        def _(i):
            c = j * per_part + i
            rows = pl.ds(first_row(c), chunk)
            here = pl.ds(pl.multiple_of(i * chunk, chunk), chunk)
            levels = [local_lse[rows, :]]
            for p in range(1, pages):
                send_lse(p, c).wait_recv()
                send_out(p, c).wait_recv()
                tile = jnp.concatenate(
                    [lse_in[p - 1, c], jnp.zeros((LANES - 8, LANES), F32)], axis=0
                )
                levels.append(tile.T[:chunk])
            largest = functools.reduce(jnp.maximum, levels)
            factors = [jnp.exp2(level - largest) for level in levels]
            inverse = 1.0 / functools.reduce(jnp.add, factors)
            factors = [factor * inverse for factor in factors]
            for h in range(heads):
                columns = slice(h * HD, (h + 1) * HD)
                total = factors[0][:, h : h + 1] * local_out[rows, columns]
                for p in range(1, pages):
                    term = out_in[p - 1, rows, columns].astype(F32)
                    total = total + factors[p][:, h : h + 1] * term
                attention[here, columns] = total.astype(BF16)

        target = proj_send.at[j] if j < n_tp - 1 else own
        tile_width = min(features, 1024)

        @pl.loop(0, features // tile_width)
        def _(t):
            columns = pl.ds(pl.multiple_of(t * tile_width, tile_width), tile_width)
            target[:, columns] = dot(attention[...], w[:, columns]).astype(BF16)

        if j < n_tp - 1:
            send_proj(j).start()

    for j in range(n_tp - 1):
        send_proj(j).wait_recv()

    @pl.loop(0, part // 16)
    def _(i):
        rows = pl.ds(pl.multiple_of(i * 16, 16), 16)
        summed = own[rows, :].astype(F32)
        for j in range(n_tp - 1):
            summed = summed + proj_in[j, rows, :].astype(F32)
        hidden = (residual[rows, :].astype(F32) + summed).astype(BF16)
        hidden_ref[rows, :] = hidden
        wide = hidden.astype(F32)
        mean = jnp.sum(wide * wide, axis=1, keepdims=True) * (1.0 / features)
        normed_ref[rows, :] = (wide * lax.rsqrt(mean + 1e-05) * gain_ref[...]).astype(BF16)

    for p in range(1, pages):
        send_lens(p).wait_send()

    @pl.loop(0, chunks)
    def _(c):
        for p in range(1, pages):
            send_q(p, c).wait_send()
            send_lse(p, c).wait_send()
            send_out(p, c).wait_send()

    for j in range(n_tp - 1):
        send_proj(j).wait_send()


def per_device(n_req, n_tp, queries, new_kv, kv_pool, cache_lens, parents, accepted, residual, w_out, norm_gain):
    requests, pages, page, row_width = kv_pool.shape
    tokens, width = queries.shape
    features = w_out.shape[1]
    part = tokens // n_tp
    chunk = min(part, 2 * TREE)
    chunks = tokens // chunk
    away = pages - 1
    vmem = pl.BlockSpec(memory_space=pltpu.VMEM)
    smem = pl.BlockSpec(memory_space=pltpu.SMEM)
    hbm = pl.BlockSpec(memory_space=pl.ANY)
    dma = pltpu.SemaphoreType.DMA
    hidden_out, normed, path = pl.pallas_call(
        functools.partial(kernel, n_req, n_tp, chunk),
        out_shape=(
            jax.ShapeDtypeStruct((part, features), BF16),
            jax.ShapeDtypeStruct((part, features), BF16),
            jax.ShapeDtypeStruct((requests * PATH, row_width), BF16),
        ),
        in_specs=[smem, smem, vmem, vmem, vmem, hbm, hbm, hbm, vmem],
        out_specs=(vmem, vmem, vmem),
        scratch_shapes=[
            pltpu.VMEM((pages, requests, page, row_width), BF16),
            pltpu.VMEM(w_out.shape, BF16),
            pltpu.VMEM((part, features), BF16),
            pltpu.VMEM((away, tokens, width), BF16),
            pltpu.VMEM((requests, LANES), jnp.int32),
            pltpu.VMEM((away, requests, LANES), jnp.int32),
            pltpu.VMEM((away, tokens, width), BF16),
            pltpu.VMEM((away, tokens, width), BF16),
            pltpu.VMEM((away, chunks, 8, LANES), F32),
            pltpu.VMEM((away, chunks, 8, LANES), F32),
            pltpu.VMEM((tokens, width), F32),
            pltpu.VMEM((tokens, LANES), F32),
            pltpu.VMEM((LANES, LANES), F32),
            pltpu.VMEM((tokens, TREE), F32),
            pltpu.VMEM((part, width), BF16),
            pltpu.VMEM((part, features), BF16),
            pltpu.VMEM((max(n_tp - 1, 1), part, features), BF16),
            pltpu.VMEM((max(n_tp - 1, 1), part, features), BF16),
            dma((pages + 2,)),
            dma((away,)),
            dma((away,)),
            dma((away, chunks)),
            dma((away, chunks)),
            dma((away, chunks)),
            dma((away, chunks)),
            dma((away, chunks)),
            dma((away, chunks)),
            dma((max(n_tp - 1, 1),)),
            dma((max(n_tp - 1, 1),)),
        ],
        compiler_params=pltpu.CompilerParams(
            collective_id=0, has_side_effects=True, vmem_limit_bytes=56 * 2**20
        ),
    )(
        cache_lens, accepted, parents, queries, new_kv, kv_pool, residual, w_out,
        norm_gain.reshape(1, features),
    )
    return hidden_out, normed, path.reshape(requests, PATH, row_width)


def solution(mesh):
    placed = (
        P("req", "tp"),
        P("req", "tp"),
        P("req", None, None, "tp"),
        P("req"),
        P("req", None),
        P("req"),
        P(("req", "tp"), None),
        P("tp", None),
        P(),
    )
    return jax.shard_map(
        functools.partial(per_device, mesh.shape["req"], mesh.shape["tp"]),
        mesh=mesh,
        in_specs=placed,
        out_specs=(P(("req", "tp"), None), P(("req", "tp"), None), P("req", None, "tp")),
        check_vma=False,
    )
```

time: 348 us -> 76.7 us (0.22)
  waiting for transfers between devices: 249 us -> 0 us
  Pallas kernels: 0 us -> 69.7 us
  local copies, waits for them, and re-layouts: 41.1 us -> 6.14 us
  matrix products: 26 us -> 0 us
  between operations: 14.3 us -> 0.64 us
  starting transfers between devices: 8.85 us -> 0 us
  other arithmetic: 8 us -> 0 us
    ppermute x3 -> x0, waiting for transfers between devices: 239 us -> none  [shifted(): return lax.ppermute(value, axis, pairs)]
    pallas_call x0 -> x1, Pallas kernels: none -> 69.7 us  [per_device(): pl.pallas_call(functools.partial(kernel, n_req, n_tp, chunk), out_shape=(...]
    dot_general x12 -> x0, matrix products: 26 us -> none  [the longest x5 9.78 us: block_partial(): jnp.einsum('rtkgc,rckd->rtkgd', weights.astype(jnp.bfloat16), value_rows,...]
    unnamed x22 -> x3, local copies, waits for them, and re-layouts: 26.7 us -> 6.14 us
    slice x2 -> x0, local copies, waits for them, and re-layouts: 12.9 us -> none  [the longest x1 12.2 us: per_device(): page_rows = kv_pool[:, page_index]]
    reduce_scatter x1 -> x0, waiting for transfers between devices: 9.74 us -> none  [per_device(): lax.psum_scatter(lax.optimization_barrier(product.astype(jnp.bfloat16)).a...]
    ppermute x3 -> x0, starting transfers between devices: 8.82 us -> none  [shifted(): return lax.ppermute(value, axis, pairs)]
    reduce_sum x12 -> x0, other arithmetic: 6.08 us -> none  [the longest x3 3.4 us: block_partial(): totals = jnp.sum(weights, axis=-1)]
  transfers between devices with their start and end apart: 4 -> 0, of which waited for: 4 -> 0; matrix products, arithmetic and copies ran while one was open for 9% -> 0% of each run, Pallas kernels for 0% -> 0%
where the time goes in v1:
time: 76.7 us; the launch traced here: 76.5 us
  Pallas kernels  69.7 us (91%)
  local copies, waits for them, and re-layouts  6.14 us (8%)
    pallas_call x1, Pallas kernels, per_device(): pl.pallas_call(functools.partial(kernel, n_req, n_tp, chunk), out_shape=(...  69.7 us
    unnamed x3, local copies, waits for them, and re-layouts  6.14 us

profile of v1, /device:TPU:0, one launch (start us, length us, event | category | flops | bytes accessed | tf_op | source)
XLA Modules:
  0.0 76.5 jit_solution(814662387041416128)
XLA Ops:
  0.6 69.7 %shard_map.112 = (bf16[128,4096]{1,0:T(8,128)(2,1)}, bf16[128,4096]{1,0:T(8,128)(2,1)}, bf16[64,1024]{1,0:T(8,128)(2,1)}) custom-call(s32[8]{0:T(128)} %lens_s.1, s32[8]{0:T(128)} %accepted_s.1, s32[8,32]{1,0:T(8,128)} %parents_ref.1, bf16[256,1024]{1,0:T(8,128)(2,1)} %q_ref.1, bf16[256,1024]{1,0:T(8,128)(2,1)} %fresh_ref.1, ...), custom_call_target="tpu_custom_call" | custom-call | tf_op jit(solution)/shard_map/pallas_call | solution.py:330
  70.3 2.3 %copy.15 = bf16[128,4096]{1,0:T(8,128)(2,1)} copy(bf16[128,4096]{1,0:T(8,128)(2,1)} %get-tuple-element.12) | data formatting | bytes 2097152
  72.6 2.3 %copy.16 = bf16[128,4096]{1,0:T(8,128)(2,1)} copy(bf16[128,4096]{1,0:T(8,128)(2,1)} %get-tuple-element.13) | data formatting | bytes 2097152
  74.9 1.6 %copy.17 = bf16[8,8,1024]{2,1,0:T(8,128)(2,1)} copy(bf16[8,8,1024]{2,1,0:T(8,128)(2,1)} %bitcast.2) | data formatting | bytes 262144

commit v2 on v1

--- a/solution.py
+++ b/solution.py
@@ -54,10 +54,10 @@
 
 def kernel(
     n_req, n_tp, chunk,
-    lens_s, accepted_s, parents_ref, q_ref, fresh_ref, kv_hbm, residual_hbm, w_hbm, gain_ref,
-    hidden_ref, normed_ref, path_ref,
+    lens_s, accepted_s, parents_ref, q_ref, fresh_ref, kv_hbm, residual_hbm, w_hbm,
+    hidden_ref, path_ref,
     kv, w, residual, q_in, lens_own, lens_in, out_send, out_in, lse_send, lse_in,
-    local_out, local_lse, lse_tile, tree, attention, own, proj_send, proj_in,
+    local_out, local_lse, lse_tile, tree, attention, proj_send, proj_in,
     load_sem, lens_send_sem, lens_recv_sem, q_send_sem, q_recv_sem, o_send_sem, o_recv_sem,
     l_send_sem, l_recv_sem, p_send_sem, p_recv_sem,
 ):
@@ -174,37 +174,111 @@
         wide = jnp.concatenate([row] * (page // LANES), axis=1)
         return iota((1, page), 1) + p * page < wide
 
-    loads[0].wait()
-
-    @pl.loop(0, requests)
-    def _(r):
-        rows = pl.ds(pl.multiple_of(r * TREE, TREE), TREE)
-        valid = lens_mask(lens_own[pl.ds(r, 1), :], 0)
-        allowed = jnp.concatenate([tree[rows, :]] * group, axis=0) > 0.0
+    ones = jnp.ones((page, HD), BF16)
+    units = [(i, k) for i in range(chunk // TREE) for k in range(kv_heads)]
+
+    def key_columns(k):
+        return slice(2 * k * HD, (2 * k + 1) * HD)
+
+    def value_columns(k):
+        return slice((2 * k + 1) * HD, (2 * k + 2) * HD)
+
+    def with_ones(value_rows):
+        return jnp.concatenate([value_rows, ones[: value_rows.shape[0]]], axis=1)
+
+    def by_token(levels, i):
         lse = jnp.zeros((TREE, LANES), F32)
         for k in range(kv_heads):
-            keys = slice(2 * k * HD, (2 * k + 1) * HD)
-            values = slice((2 * k + 1) * HD, (2 * k + 2) * HD)
-            query = stacked_queries(q_ref, rows, k)
-            cached = jnp.where(valid, dot_t(query, kv[0, r, :, keys]) * SCALE2, NEGATIVE)
-            drafted = jnp.where(allowed, dot_t(query, fresh_ref[rows, keys]) * SCALE2, NEGATIVE)
-            largest = jnp.maximum(
-                jnp.max(cached, axis=1, keepdims=True), jnp.max(drafted, axis=1, keepdims=True)
+            for g in range(group):
+                level = levels[i * kv_heads + k][g * TREE : (g + 1) * TREE]
+                lse = jnp.where(lane == k * group + g, level, lse)
+        return lse
+
+    def token_rows(start, i):
+        return pl.ds(pl.multiple_of(start + i * TREE, TREE), TREE)
+
+    def local_chunk(start):
+        first = start // TREE
+        valid = [lens_mask(lens_own[pl.ds(first + i, 1), :], 0) for i in range(chunk // TREE)]
+        allowed = [
+            jnp.concatenate([tree[token_rows(start, i), :]] * group, axis=0) > 0.0
+            for i in range(chunk // TREE)
+        ]
+        queries = [stacked_queries(q_ref, token_rows(start, i), k) for i, k in units]
+        cached = [
+            jnp.where(valid[i], dot_t(query, kv[0, first + i, :, key_columns(k)]) * SCALE2, NEGATIVE)
+            for query, (i, k) in zip(queries, units)
+        ]
+        drafted = [
+            jnp.where(
+                allowed[i],
+                dot_t(query, fresh_ref[token_rows(start, i), key_columns(k)]) * SCALE2,
+                NEGATIVE,
             )
-            cached = jnp.exp2(cached - largest)
-            drafted = jnp.exp2(drafted - largest)
-            total = jnp.sum(cached, axis=1, keepdims=True) + jnp.sum(drafted, axis=1, keepdims=True)
-            out = dot(cached.astype(BF16), kv[0, r, :, values])
-            out = out + dot(drafted.astype(BF16), fresh_ref[rows, values])
-            out = out / total
-            level = largest + jnp.log2(total)
+            for query, (i, k) in zip(queries, units)
+        ]
+        largest = [
+            jnp.maximum(jnp.max(old, axis=1, keepdims=True), jnp.max(new, axis=1, keepdims=True))
+            for old, new in zip(cached, drafted)
+        ]
+        cached = [jnp.exp2(old - top).astype(BF16) for old, top in zip(cached, largest)]
+        drafted = [jnp.exp2(new - top).astype(BF16) for new, top in zip(drafted, largest)]
+        sums = [
+            dot(old, with_ones(kv[0, first + i, :, value_columns(k)]))
+            + dot(new, with_ones(fresh_ref[token_rows(start, i), value_columns(k)]))
+            for old, new, (i, k) in zip(cached, drafted, units)
+        ]
+        levels = []
+        for both, top, (i, k) in zip(sums, largest, units):
+            total = both[:, HD:]
+            out = both[:, :HD] / total
+            levels.append(top + jnp.log2(total))
             for g in range(group):
                 h = k * group + g
-                some = slice(g * TREE, (g + 1) * TREE)
-                local_out[rows, h * HD : (h + 1) * HD] = out[some]
-                lse = jnp.where(lane == h, level[some], lse)
-        local_lse[rows, :] = lse
-
+                local_out[token_rows(start, i), h * HD : (h + 1) * HD] = out[g * TREE : (g + 1) * TREE]
+        for i in range(chunk // TREE):
+            local_lse[token_rows(start, i), :] = by_token(levels, i)
+
+    def remote_chunk(start, c, p):
+        first = start // TREE
+        valid = [lens_mask(lens_in[p - 1, pl.ds(first + i, 1), :], p) for i in range(chunk // TREE)]
+        cached = [
+            jnp.where(
+                valid[i],
+                dot_t(
+                    stacked_queries(q_in.at[p - 1], token_rows(start, i), k),
+                    kv[p, first + i, :, key_columns(k)],
+                )
+                * SCALE2,
+                NEGATIVE,
+            )
+            for i, k in units
+        ]
+        largest = [jnp.max(scores, axis=1, keepdims=True) for scores in cached]
+        cached = [
+            jnp.exp2(scores - jnp.maximum(top, FLOOR)).astype(BF16)
+            for scores, top in zip(cached, largest)
+        ]
+        sums = [
+            dot(weights, with_ones(kv[p, first + i, :, value_columns(k)]))
+            for weights, (i, k) in zip(cached, units)
+        ]
+        levels = []
+        for both, top, (i, k) in zip(sums, largest, units):
+            total = jnp.maximum(both[:, HD:], 1.0)
+            out = (both[:, :HD] / total).astype(BF16)
+            levels.append(top + jnp.log2(total))
+            for g in range(group):
+                h = k * group + g
+                out_send[p - 1, token_rows(start, i), h * HD : (h + 1) * HD] = out[
+                    g * TREE : (g + 1) * TREE
+                ]
+        for i in range(chunk // TREE):
+            lse_tile[i * TREE : (i + 1) * TREE, :] = by_token(levels, i)
+        lse_send[p - 1, c] = lse_tile[...].T[:8]
+
+    loads[0].wait()
+    local_chunk(first_row(0))
     for p in range(1, pages):
         loads[p].wait()
         send_lens(p).wait_recv()
@@ -214,36 +288,13 @@
         start = first_row(c)
         for p in range(1, pages):
             send_q(p, c).wait_recv()
-
-            @pl.loop(0, chunk // TREE)
-            def _(i):
-                r = start // TREE + i
-                rows = pl.ds(pl.multiple_of(start + i * TREE, TREE), TREE)
-                valid = lens_mask(lens_in[p - 1, pl.ds(r, 1), :], p)
-                lse = jnp.zeros((TREE, LANES), F32)
-                for k in range(kv_heads):
-                    keys = slice(2 * k * HD, (2 * k + 1) * HD)
-                    values = slice((2 * k + 1) * HD, (2 * k + 2) * HD)
-                    query = stacked_queries(q_in.at[p - 1], rows, k)
-                    cached = jnp.where(valid, dot_t(query, kv[p, r, :, keys]) * SCALE2, NEGATIVE)
-                    largest = jnp.max(cached, axis=1, keepdims=True)
-                    cached = jnp.exp2(cached - jnp.maximum(largest, FLOOR))
-                    total = jnp.sum(cached, axis=1, keepdims=True)
-                    out = dot(cached.astype(BF16), kv[p, r, :, values])
-                    some_valid = total > 0.0
-                    safe = jnp.where(some_valid, total, 1.0)
-                    out = out / safe
-                    level = jnp.where(some_valid, largest + jnp.log2(safe), NEGATIVE)
-                    for g in range(group):
-                        h = k * group + g
-                        some = slice(g * TREE, (g + 1) * TREE)
-                        out_send[p - 1, rows, h * HD : (h + 1) * HD] = out[some].astype(BF16)
-                        lse = jnp.where(lane == h, level[some], lse)
-                lse_tile[pl.ds(pl.multiple_of(i * TREE, TREE), TREE), :] = lse
-
-            lse_send[p - 1, c] = lse_tile[...].T[:8]
+            remote_chunk(start, c, p)
             send_lse(p, c).start()
             send_out(p, c).start()
+
+        @pl.when(c < chunks - 1)
+        def _():
+            local_chunk(first_row(c + 1))
 
     loads[pages].wait()
     loads[pages + 1].wait()
@@ -275,31 +326,25 @@
                     total = total + factors[p][:, h : h + 1] * term
                 attention[here, columns] = total.astype(BF16)
 
-        target = proj_send.at[j] if j < n_tp - 1 else own
+        if j == n_tp - 1:
+            for other in range(n_tp - 1):
+                send_proj(other).wait_recv()
         tile_width = min(features, 1024)
 
         @pl.loop(0, features // tile_width)
         def _(t):
             columns = pl.ds(pl.multiple_of(t * tile_width, tile_width), tile_width)
-            target[:, columns] = dot(attention[...], w[:, columns]).astype(BF16)
+            projected = dot(attention[...], w[:, columns]).astype(BF16)
+            if j < n_tp - 1:
+                proj_send[j, :, columns] = projected
+            else:
+                summed = projected.astype(F32)
+                for other in range(n_tp - 1):
+                    summed = summed + proj_in[other, :, columns].astype(F32)
+                hidden_ref[:, columns] = (residual[:, columns].astype(F32) + summed).astype(BF16)
 
         if j < n_tp - 1:
             send_proj(j).start()
-
-    for j in range(n_tp - 1):
-        send_proj(j).wait_recv()
-
-    @pl.loop(0, part // 16)
-    def _(i):
-        rows = pl.ds(pl.multiple_of(i * 16, 16), 16)
-        summed = own[rows, :].astype(F32)
-        for j in range(n_tp - 1):
-            summed = summed + proj_in[j, rows, :].astype(F32)
-        hidden = (residual[rows, :].astype(F32) + summed).astype(BF16)
-        hidden_ref[rows, :] = hidden
-        wide = hidden.astype(F32)
-        mean = jnp.sum(wide * wide, axis=1, keepdims=True) * (1.0 / features)
-        normed_ref[rows, :] = (wide * lax.rsqrt(mean + 1e-05) * gain_ref[...]).astype(BF16)
 
     for p in range(1, pages):
         send_lens(p).wait_send()
@@ -313,6 +358,15 @@
 
     for j in range(n_tp - 1):
         send_proj(j).wait_send()
+
+
+def norm_kernel(hidden_ref, gain_ref, path_ref, hidden_out, normed_out, path_out):
+    hidden = hidden_ref[...]
+    hidden_out[...] = hidden
+    wide = hidden.astype(F32)
+    mean = jnp.sum(wide * wide, axis=1, keepdims=True) * (1.0 / wide.shape[1])
+    normed_out[...] = (wide * lax.rsqrt(mean + 1e-05) * gain_ref[...]).astype(BF16)
+    path_out[...] = path_ref[...]
 
 
 def per_device(n_req, n_tp, queries, new_kv, kv_pool, cache_lens, parents, accepted, residual, w_out, norm_gain):
@@ -327,15 +381,14 @@
     smem = pl.BlockSpec(memory_space=pltpu.SMEM)
     hbm = pl.BlockSpec(memory_space=pl.ANY)
     dma = pltpu.SemaphoreType.DMA
-    hidden_out, normed, path = pl.pallas_call(
+    hidden, path = pl.pallas_call(
         functools.partial(kernel, n_req, n_tp, chunk),
         out_shape=(
             jax.ShapeDtypeStruct((part, features), BF16),
-            jax.ShapeDtypeStruct((part, features), BF16),
             jax.ShapeDtypeStruct((requests * PATH, row_width), BF16),
         ),
-        in_specs=[smem, smem, vmem, vmem, vmem, hbm, hbm, hbm, vmem],
-        out_specs=(vmem, vmem, vmem),
+        in_specs=[smem, smem, vmem, vmem, vmem, hbm, hbm, hbm],
+        out_specs=(vmem, vmem),
         scratch_shapes=[
             pltpu.VMEM((pages, requests, page, row_width), BF16),
             pltpu.VMEM(w_out.shape, BF16),
@@ -352,7 +405,6 @@
             pltpu.VMEM((LANES, LANES), F32),
             pltpu.VMEM((tokens, TREE), F32),
             pltpu.VMEM((part, width), BF16),
-            pltpu.VMEM((part, features), BF16),
             pltpu.VMEM((max(n_tp - 1, 1), part, features), BF16),
             pltpu.VMEM((max(n_tp - 1, 1), part, features), BF16),
             dma((pages + 2,)),
@@ -370,10 +422,21 @@
         compiler_params=pltpu.CompilerParams(
             collective_id=0, has_side_effects=True, vmem_limit_bytes=56 * 2**20
         ),
-    )(
-        cache_lens, accepted, parents, queries, new_kv, kv_pool, residual, w_out,
-        norm_gain.reshape(1, features),
-    )
+    )(cache_lens, accepted, parents, queries, new_kv, kv_pool, residual, w_out)
+    rows = min(part, TREE)
+    row_block = pl.BlockSpec((rows, features), lambda i: (i, 0))
+    whole_path = pl.BlockSpec(path.shape, lambda i: (0, 0))
+    hidden_out, normed, path = pl.pallas_call(
+        norm_kernel,
+        grid=(part // rows,),
+        out_shape=(
+            jax.ShapeDtypeStruct(hidden.shape, BF16),
+            jax.ShapeDtypeStruct(hidden.shape, BF16),
+            jax.ShapeDtypeStruct(path.shape, BF16),
+        ),
+        in_specs=[row_block, pl.BlockSpec((1, features), lambda i: (0, 0)), whole_path],
+        out_specs=(row_block, row_block, whole_path),
+    )(hidden, norm_gain.reshape(1, features), path)
     return hidden_out, normed, path.reshape(requests, PATH, row_width)
 
 

time: 76.7 us -> 72.6 us (0.947)
  local copies, waits for them, and re-layouts: 6.14 us -> 0 us
  Pallas kernels: 69.7 us -> 71.8 us
    unnamed x3 -> x0, local copies, waits for them, and re-layouts: 6.14 us -> none
    pallas_call x0 -> x1, Pallas kernels: none -> 3.77 us  [per_device(): pl.pallas_call(norm_kernel, grid=(part // rows,), out_shape=(jax.ShapeDty...]
    pallas_call x1, Pallas kernels: 69.7 us -> 68 us  [per_device(): pl.pallas_call(functools.partial(kernel, n_req, n_tp, chunk), out_shape=(...]
where the time goes in v2:
time: 72.6 us; the launch traced here: 72.4 us
  Pallas kernels  71.8 us (99%)
    pallas_call x1, Pallas kernels, per_device(): pl.pallas_call(functools.partial(kernel, n_req, n_tp, chunk), out_shape=(...  68 us
    pallas_call x1, Pallas kernels, per_device(): pl.pallas_call(norm_kernel, grid=(part // rows,), out_shape=(jax.ShapeDty...  3.77 us

profile of v2, /device:TPU:0, one launch (start us, length us, event | category | flops | bytes accessed | tf_op | source)
XLA Modules:
  0.0 72.4 jit_solution(3638877236437853342)
XLA Ops:
  0.6 68.0 %shard_map.112 = (bf16[128,4096]{1,0:T(8,128)(2,1)}, bf16[64,1024]{1,0:T(8,128)(2,1)}) custom-call(s32[8]{0:T(128)} %lens_s.1, s32[8]{0:T(128)} %accepted_s.1, s32[8,32]{1,0:T(8,128)} %parents_ref.1, bf16[256,1024]{1,0:T(8,128)(2,1)} %q_ref.1, bf16[256,1024]{1,0:T(8,128)(2,1)} %fresh_ref.1, bf16[8,4,256,1024]{3,2,1,0:T(8,128)(2,1)} %kv_hbm.1, ...), custom_call_target="tpu_custom_call" | custom-call | tf_op jit(solution)/shard_map/pallas_call | solution.py:384
  68.7 3.8 %shard_map.113 = (bf16[128,4096]{1,0:T(8,128)(2,1)}, bf16[128,4096]{1,0:T(8,128)(2,1)}, bf16[64,1024]{1,0:T(8,128)(2,1)}) custom-call(bf16[128,4096]{1,0:T(8,128)(2,1)} %get-tuple-element.8.hidden_ref, f32[1,4096]{1,0:T(1,128)} %bitcast.2, bf16[64,1024]{1,0:T(8,128)(2,1)} %get-tuple-element.9.path_ref), custom_call_target="tpu_custom_call" | custom-call | tf_op jit(solution)/shard_map/pallas_call | solution.py:429

commit v3 on v2

--- a/solution.py
+++ b/solution.py
@@ -58,8 +58,11 @@
     hidden_ref, path_ref,
     kv, w, residual, q_in, lens_own, lens_in, out_send, out_in, lse_send, lse_in,
     local_out, local_lse, lse_tile, tree, attention, proj_send, proj_in,
+    q_relay, lens_relay, out_relay, out_far, lse_relay, lse_far,
     load_sem, lens_send_sem, lens_recv_sem, q_send_sem, q_recv_sem, o_send_sem, o_recv_sem,
     l_send_sem, l_recv_sem, p_send_sem, p_recv_sem,
+    zn_send_sem, zn_recv_sem, zq_send_sem, zq_recv_sem, zo_send_sem, zo_recv_sem,
+    zl_send_sem, zl_recv_sem,
 ):
     me, tp = lax.axis_index("req"), lax.axis_index("tp")
     tokens, width = q_ref.shape
@@ -81,16 +84,26 @@
     for load in loads:
         load.start()
 
+    place = lax.rem(me, pages)
+    layer = me - place
+    above = lax.rem(me + pages, n_req)
+    below = lax.rem(me + n_req - pages, n_req)
+
     def ahead(p):
-        return lax.rem(me + p, n_req)
+        return layer + lax.rem(place + p, pages)
 
     def behind(p):
-        return lax.rem(me + n_req - p, n_req)
+        return layer + lax.rem(place + pages - p, pages)
+
+    def if_near(p, action):
+        pl.when(place + p < pages)(action)
+
+    def if_far(p, action):
+        pl.when(place + p >= pages)(action)
 
     barrier = pltpu.get_barrier_semaphore()
-    for p in range(1, pages):
-        for other in (ahead(p), behind(p)):
-            pl.semaphore_signal(barrier, inc=1, device_id={"req": other}, device_id_type=MESH)
+    for other in [ahead(p) for p in range(1, pages)] + [above, below]:
+        pl.semaphore_signal(barrier, inc=1, device_id={"req": other}, device_id_type=MESH)
     for j in range(1, n_tp):
         pl.semaphore_signal(
             barrier, inc=1, device_id={"tp": lax.rem(tp + j, n_tp)}, device_id_type=MESH
@@ -100,22 +113,22 @@
     for r in range(requests):
         lens = jnp.where(iota((requests, LANES), 0) == r, lens_s[r], lens)
     lens_own[...] = lens
-    pl.semaphore_wait(barrier, 2 * (pages - 1) + n_tp - 1)
+    pl.semaphore_wait(barrier, pages + 1 + n_tp - 1)
 
     def first_row(c):
         block = lax.rem(tp + 1 + c // per_part, n_tp)
         return pl.multiple_of(block * part + lax.rem(c, per_part) * chunk, chunk)
 
-    def send_lens(p):
-        return pltpu.make_async_remote_copy(
-            lens_own, lens_in.at[p - 1], lens_send_sem.at[p - 1], lens_recv_sem.at[p - 1],
+    def send_lens(p, source=lens_own):
+        return pltpu.make_async_remote_copy(
+            source, lens_in.at[p - 1], lens_send_sem.at[p - 1], lens_recv_sem.at[p - 1],
             device_id={"req": ahead(p)}, device_id_type=MESH,
         )
 
-    def send_q(p, c):
+    def send_q(p, c, source=q_ref):
         rows = pl.ds(first_row(c), chunk)
         return pltpu.make_async_remote_copy(
-            q_ref.at[rows], q_in.at[p - 1, rows], q_send_sem.at[p - 1, c], q_recv_sem.at[p - 1, c],
+            source.at[rows], q_in.at[p - 1, rows], q_send_sem.at[p - 1, c], q_recv_sem.at[p - 1, c],
             device_id={"req": ahead(p)}, device_id_type=MESH,
         )
 
@@ -140,13 +153,46 @@
             device_id={"tp": lax.rem(tp + 1 + j, n_tp)}, device_id_type=MESH,
         )
 
+    def cross_lens():
+        return pltpu.make_async_remote_copy(
+            lens_own, lens_relay, zn_send_sem, zn_recv_sem,
+            device_id={"req": above}, device_id_type=MESH,
+        )
+
+    def cross_q(c):
+        rows = pl.ds(first_row(c), chunk)
+        return pltpu.make_async_remote_copy(
+            q_ref.at[rows], q_relay.at[rows], zq_send_sem.at[c], zq_recv_sem.at[c],
+            device_id={"req": above}, device_id_type=MESH,
+        )
+
+    def cross_out(c):
+        rows = pl.ds(first_row(c), chunk)
+        return pltpu.make_async_remote_copy(
+            out_relay.at[rows], out_far.at[rows], zo_send_sem.at[c], zo_recv_sem.at[c],
+            device_id={"req": below}, device_id_type=MESH,
+        )
+
+    def cross_lse(c):
+        return pltpu.make_async_remote_copy(
+            lse_relay.at[c], lse_far.at[c], zl_send_sem.at[c], zl_recv_sem.at[c],
+            device_id={"req": below}, device_id_type=MESH,
+        )
+
+    cross_lens().start()
     for p in range(1, pages):
-        send_lens(p).start()
+        if_near(p, lambda p=p: send_lens(p).start())
 
     @pl.loop(0, chunks)
     def _(c):
+        cross_q(c).start()
         for p in range(1, pages):
-            send_q(p, c).start()
+            if_near(p, lambda p=p: send_q(p, c).start())
+
+    def pass_on(c):
+        cross_q(c).wait_recv()
+        for p in range(1, pages):
+            if_far(p, lambda p=p: send_q(p, c, q_relay).start())
 
     marked = tree_masks(parents_ref[...], tokens)
     fold = indicator((iota((tokens, TREE), 0) & (TREE - 1)) == iota((tokens, TREE), 1))
@@ -277,6 +323,42 @@
             lse_tile[i * TREE : (i + 1) * TREE, :] = by_token(levels, i)
         lse_send[p - 1, c] = lse_tile[...].T[:8]
 
+    def by_row(compact):
+        tile = jnp.concatenate([compact, jnp.zeros((LANES - 8, LANES), F32)], axis=0)
+        return tile.T[:chunk]
+
+    def near_levels(c, near):
+        levels = []
+        for p in range(1, pages):
+            wanted = (place + p < pages) if near else (place + p >= pages)
+            levels.append(jnp.where(wanted, lse_in[p - 1, c], NEGATIVE))
+        return levels
+
+    def merge_far(c):
+        rows = pl.ds(first_row(c), chunk)
+        for p in range(1, pages):
+            send_lse(p, c).wait_recv()
+            send_out(p, c).wait_recv()
+        levels = near_levels(c, False)
+        largest = functools.reduce(jnp.maximum, levels)
+        factors = [jnp.exp2(level - largest) for level in levels]
+        total = functools.reduce(jnp.add, factors)
+        lse_relay[c] = largest + jnp.log2(total)
+        factors = [by_row(factor / total) for factor in factors]
+        for h in range(heads):
+            columns = slice(h * HD, (h + 1) * HD)
+            terms = [
+                factors[p - 1][:, h : h + 1] * out_in[p - 1, rows, columns].astype(F32)
+                for p in range(1, pages)
+            ]
+            out_relay[rows, columns] = functools.reduce(jnp.add, terms).astype(BF16)
+        cross_lse(c).start()
+        cross_out(c).start()
+
+    cross_lens().wait_recv()
+    for p in range(1, pages):
+        if_far(p, lambda p=p: send_lens(p, lens_relay).start())
+    pass_on(0)
     loads[0].wait()
     local_chunk(first_row(0))
     for p in range(1, pages):
@@ -286,6 +368,11 @@
     @pl.loop(0, chunks)
     def _(c):
         start = first_row(c)
+
+        @pl.when(c < chunks - 1)
+        def _():
+            pass_on(c + 1)
+
         for p in range(1, pages):
             send_q(p, c).wait_recv()
             remote_chunk(start, c, p)
@@ -296,6 +383,12 @@
         def _():
             local_chunk(first_row(c + 1))
 
+        @pl.when(c > 0)
+        def _():
+            merge_far(c - 1)
+
+    merge_far(chunks - 1)
+
     loads[pages].wait()
     loads[pages + 1].wait()
 
@@ -306,14 +399,10 @@
             c = j * per_part + i
             rows = pl.ds(first_row(c), chunk)
             here = pl.ds(pl.multiple_of(i * chunk, chunk), chunk)
-            levels = [local_lse[rows, :]]
-            for p in range(1, pages):
-                send_lse(p, c).wait_recv()
-                send_out(p, c).wait_recv()
-                tile = jnp.concatenate(
-                    [lse_in[p - 1, c], jnp.zeros((LANES - 8, LANES), F32)], axis=0
-                )
-                levels.append(tile.T[:chunk])
+            cross_lse(c).wait_recv()
+            cross_out(c).wait_recv()
+            levels = [local_lse[rows, :], by_row(lse_far[c])]
+            levels += [by_row(level) for level in near_levels(c, True)]
             largest = functools.reduce(jnp.maximum, levels)
             factors = [jnp.exp2(level - largest) for level in levels]
             inverse = 1.0 / functools.reduce(jnp.add, factors)
@@ -321,9 +410,10 @@
             for h in range(heads):
                 columns = slice(h * HD, (h + 1) * HD)
                 total = factors[0][:, h : h + 1] * local_out[rows, columns]
-                for p in range(1, pages):
-                    term = out_in[p - 1, rows, columns].astype(F32)
-                    total = total + factors[p][:, h : h + 1] * term
+                terms = [out_far[rows, columns]]
+                terms += [out_in[p - 1, rows, columns] for p in range(1, pages)]
+                for factor, term in zip(factors[1:], terms):
+                    total = total + factor[:, h : h + 1] * term.astype(F32)
                 attention[here, columns] = total.astype(BF16)
 
         if j == n_tp - 1:
@@ -349,8 +439,13 @@
     for p in range(1, pages):
         send_lens(p).wait_send()
 
+    cross_lens().wait_send()
+
     @pl.loop(0, chunks)
     def _(c):
+        cross_q(c).wait_send()
+        cross_lse(c).wait_send()
+        cross_out(c).wait_send()
         for p in range(1, pages):
             send_q(p, c).wait_send()
             send_lse(p, c).wait_send()
@@ -407,6 +502,12 @@
             pltpu.VMEM((part, width), BF16),
             pltpu.VMEM((max(n_tp - 1, 1), part, features), BF16),
             pltpu.VMEM((max(n_tp - 1, 1), part, features), BF16),
+            pltpu.VMEM((tokens, width), BF16),
+            pltpu.VMEM((requests, LANES), jnp.int32),
+            pltpu.VMEM((tokens, width), BF16),
+            pltpu.VMEM((tokens, width), BF16),
+            pltpu.VMEM((chunks, 8, LANES), F32),
+            pltpu.VMEM((chunks, 8, LANES), F32),
             dma((pages + 2,)),
             dma((away,)),
             dma((away,)),
@@ -418,6 +519,14 @@
             dma((away, chunks)),
             dma((max(n_tp - 1, 1),)),
             dma((max(n_tp - 1, 1),)),
+            dma,
+            dma,
+            dma((chunks,)),
+            dma((chunks,)),
+            dma((chunks,)),
+            dma((chunks,)),
+            dma((chunks,)),
+            dma((chunks,)),
         ],
         compiler_params=pltpu.CompilerParams(
             collective_id=0, has_side_effects=True, vmem_limit_bytes=56 * 2**20

time: 72.6 us -> 73.3 us (level); the launches traced: 72.4 us -> 72 us
  no operation moved by 1% of the time
where the time goes in v3:
time: 73.3 us; the launch traced here: 72 us
  Pallas kernels  71.4 us (97%)
    pallas_call x1, Pallas kernels, per_device(): pl.pallas_call(functools.partial(kernel, n_req, n_tp, chunk), out_shape=(...  67.6 us
    pallas_call x1, Pallas kernels, per_device(): pl.pallas_call(norm_kernel, grid=(part // rows,), out_shape=(jax.ShapeDty...  3.77 us

profile of v3, /device:TPU:0, one launch (start us, length us, event | category | flops | bytes accessed | tf_op | source)
XLA Modules:
  0.0 72.0 jit_solution(18313501345197911622)
XLA Ops:
  0.6 67.6 %shard_map.112 = (bf16[128,4096]{1,0:T(8,128)(2,1)}, bf16[64,1024]{1,0:T(8,128)(2,1)}) custom-call(s32[8]{0:T(128)} %lens_s.1, s32[8]{0:T(128)} %accepted_s.1, s32[8,32]{1,0:T(8,128)} %parents_ref.1, bf16[256,1024]{1,0:T(8,128)(2,1)} %q_ref.1, bf16[256,1024]{1,0:T(8,128)(2,1)} %fresh_ref.1, bf16[8,4,256,1024]{3,2,1,0:T(8,128)(2,1)} %kv_hbm.1, ...), custom_call_target="tpu_custom_call" | custom-call | tf_op jit(solution)/shard_map/pallas_call | solution.py:479
  68.3 3.8 %shard_map.113 = (bf16[128,4096]{1,0:T(8,128)(2,1)}, bf16[128,4096]{1,0:T(8,128)(2,1)}, bf16[64,1024]{1,0:T(8,128)(2,1)}) custom-call(bf16[128,4096]{1,0:T(8,128)(2,1)} %get-tuple-element.8.hidden_ref, f32[1,4096]{1,0:T(1,128)} %bitcast.2, bf16[64,1024]{1,0:T(8,128)(2,1)} %get-tuple-element.9.path_ref), custom_call_target="tpu_custom_call" | custom-call | tf_op jit(solution)/shard_map/pallas_call | solution.py:538

commit v4 on v2

--- a/solution.py
+++ b/solution.py
@@ -54,10 +54,10 @@
 
 def kernel(
     n_req, n_tp, chunk,
-    lens_s, accepted_s, parents_ref, q_ref, fresh_ref, kv_hbm, residual_hbm, w_hbm,
+    lens_s, accepted_s, parents_ref, q_hbm, fresh_hbm, kv_hbm, residual_hbm, w_hbm,
     hidden_ref, path_ref,
-    kv, w, residual, q_in, lens_own, lens_in, out_send, out_in, lse_send, lse_in,
-    local_out, local_lse, lse_tile, tree, attention, proj_send, proj_in,
+    q_ref, fresh_ref, kv, w, residual, q_in, lens_own, lens_in, out_send, out_in, lse_send, lse_in,
+    local_out, local_lse, tree, attention, proj_send, proj_in,
     load_sem, lens_send_sem, lens_recv_sem, q_send_sem, q_recv_sem, o_send_sem, o_recv_sem,
     l_send_sem, l_recv_sem, p_send_sem, p_recv_sem,
 ):
@@ -73,12 +73,16 @@
     features = w.shape[1]
     group = heads // kv_heads
 
+    first_loads = [
+        pltpu.make_async_copy(fresh_hbm, fresh_ref, load_sem.at[pages + 2]),
+        pltpu.make_async_copy(q_hbm, q_ref, load_sem.at[pages + 3]),
+    ]
     loads = [
         pltpu.make_async_copy(kv_hbm.at[:, p], kv.at[p], load_sem.at[p]) for p in range(pages)
     ]
     loads.append(pltpu.make_async_copy(w_hbm, w, load_sem.at[pages]))
     loads.append(pltpu.make_async_copy(residual_hbm, residual, load_sem.at[pages + 1]))
-    for load in loads:
+    for load in first_loads + loads:
         load.start()
 
     def ahead(p):
@@ -115,7 +119,7 @@
     def send_q(p, c):
         rows = pl.ds(first_row(c), chunk)
         return pltpu.make_async_remote_copy(
-            q_ref.at[rows], q_in.at[p - 1, rows], q_send_sem.at[p - 1, c], q_recv_sem.at[p - 1, c],
+            q_hbm.at[rows], q_in.at[p - 1, rows], q_send_sem.at[p - 1, c], q_recv_sem.at[p - 1, c],
             device_id={"req": ahead(p)}, device_id_type=MESH,
         )
 
@@ -143,7 +147,9 @@
     for p in range(1, pages):
         send_lens(p).start()
 
-    @pl.loop(0, chunks)
+    upfront = chunks // 2
+
+    @pl.loop(0, upfront)
     def _(c):
         for p in range(1, pages):
             send_q(p, c).start()
@@ -162,6 +168,7 @@
     spread = indicator((iota(slots, 0) >> 3) == iota(slots, 1), F32)
     slot = (iota((requests * PATH, tokens), 0) & (PATH - 1)).astype(F32) + 1.0
     selector = (dot(spread, count) == slot) & (dot(spread, on_path) > 0.0)
+    first_loads[0].wait()
     path_ref[...] = dot(indicator(selector), fresh_ref[...]).astype(BF16)
 
     lane = iota((TREE, LANES), 1)
@@ -239,12 +246,18 @@
         for i in range(chunk // TREE):
             local_lse[token_rows(start, i), :] = by_token(levels, i)
 
-    def remote_chunk(start, c, p):
+    away = [(p, i, k) for p in range(1, pages) for i, k in units]
+
+    def remote_chunk(start, c):
         first = start // TREE
-        valid = [lens_mask(lens_in[p - 1, pl.ds(first + i, 1), :], p) for i in range(chunk // TREE)]
+        valid = {
+            (p, i): lens_mask(lens_in[p - 1, pl.ds(first + i, 1), :], p)
+            for p in range(1, pages)
+            for i in range(chunk // TREE)
+        }
         cached = [
             jnp.where(
-                valid[i],
+                valid[p, i],
                 dot_t(
                     stacked_queries(q_in.at[p - 1], token_rows(start, i), k),
                     kv[p, first + i, :, key_columns(k)],
@@ -252,7 +265,7 @@
                 * SCALE2,
                 NEGATIVE,
             )
-            for i, k in units
+            for p, i, k in away
         ]
         largest = [jnp.max(scores, axis=1, keepdims=True) for scores in cached]
         cached = [
@@ -261,10 +274,10 @@
         ]
         sums = [
             dot(weights, with_ones(kv[p, first + i, :, value_columns(k)]))
-            for weights, (i, k) in zip(cached, units)
+            for weights, (p, i, k) in zip(cached, away)
         ]
         levels = []
-        for both, top, (i, k) in zip(sums, largest, units):
+        for both, top, (p, i, k) in zip(sums, largest, away):
             total = jnp.maximum(both[:, HD:], 1.0)
             out = (both[:, :HD] / total).astype(BF16)
             levels.append(top + jnp.log2(total))
@@ -273,10 +286,13 @@
                 out_send[p - 1, token_rows(start, i), h * HD : (h + 1) * HD] = out[
                     g * TREE : (g + 1) * TREE
                 ]
-        for i in range(chunk // TREE):
-            lse_tile[i * TREE : (i + 1) * TREE, :] = by_token(levels, i)
-        lse_send[p - 1, c] = lse_tile[...].T[:8]
-
+        for p in range(1, pages):
+            some = levels[(p - 1) * len(units) : p * len(units)]
+            rows = [by_token(some, i) for i in range(chunk // TREE)]
+            rows.append(jnp.zeros((LANES - chunk, LANES), F32))
+            lse_send[p - 1, c] = jnp.concatenate(rows, axis=0).T[:8]
+
+    first_loads[1].wait()
     loads[0].wait()
     local_chunk(first_row(0))
     for p in range(1, pages):
@@ -285,10 +301,15 @@
 
     @pl.loop(0, chunks)
     def _(c):
-        start = first_row(c)
+        @pl.when(c < chunks - upfront)
+        def _():
+            for p in range(1, pages):
+                send_q(p, c + upfront).start()
+
         for p in range(1, pages):
             send_q(p, c).wait_recv()
-            remote_chunk(start, c, p)
+        remote_chunk(first_row(c), c)
+        for p in range(1, pages):
             send_lse(p, c).start()
             send_out(p, c).start()
 
@@ -374,7 +395,7 @@
     tokens, width = queries.shape
     features = w_out.shape[1]
     part = tokens // n_tp
-    chunk = min(part, 2 * TREE)
+    chunk = TREE
     chunks = tokens // chunk
     away = pages - 1
     vmem = pl.BlockSpec(memory_space=pltpu.VMEM)
@@ -387,9 +408,11 @@
             jax.ShapeDtypeStruct((part, features), BF16),
             jax.ShapeDtypeStruct((requests * PATH, row_width), BF16),
         ),
-        in_specs=[smem, smem, vmem, vmem, vmem, hbm, hbm, hbm],
+        in_specs=[smem, smem, vmem, hbm, hbm, hbm, hbm, hbm],
         out_specs=(vmem, vmem),
         scratch_shapes=[
+            pltpu.VMEM(queries.shape, BF16),
+            pltpu.VMEM(new_kv.shape, BF16),
             pltpu.VMEM((pages, requests, page, row_width), BF16),
             pltpu.VMEM(w_out.shape, BF16),
             pltpu.VMEM((part, features), BF16),
@@ -402,12 +425,11 @@
             pltpu.VMEM((away, chunks, 8, LANES), F32),
             pltpu.VMEM((tokens, width), F32),
             pltpu.VMEM((tokens, LANES), F32),
-            pltpu.VMEM((LANES, LANES), F32),
             pltpu.VMEM((tokens, TREE), F32),
             pltpu.VMEM((part, width), BF16),
             pltpu.VMEM((max(n_tp - 1, 1), part, features), BF16),
             pltpu.VMEM((max(n_tp - 1, 1), part, features), BF16),
-            dma((pages + 2,)),
+            dma((pages + 4,)),
             dma((away,)),
             dma((away,)),
             dma((away, chunks)),
@@ -423,7 +445,7 @@
             collective_id=0, has_side_effects=True, vmem_limit_bytes=56 * 2**20
         ),
     )(cache_lens, accepted, parents, queries, new_kv, kv_pool, residual, w_out)
-    rows = min(part, TREE)
+    rows = 16
     row_block = pl.BlockSpec((rows, features), lambda i: (i, 0))
     whole_path = pl.BlockSpec(path.shape, lambda i: (0, 0))
     hidden_out, normed, path = pl.pallas_call(

time: 72.6 us -> 75.5 us (1.040)
  Pallas kernels: 71.8 us -> 74.6 us
    pallas_call x1, Pallas kernels: 3.77 us -> 5.85 us  [per_device(): pl.pallas_call(norm_kernel, grid=(part // rows,), out_shape=(jax.ShapeDty...]
where the time goes in v4:
time: 75.5 us; the launch traced here: 75.2 us
  Pallas kernels  74.6 us (99%)
    pallas_call x1, Pallas kernels, per_device(): pl.pallas_call(functools.partial(kernel, n_req, n_tp, chunk), out_shape=(...  68.7 us
    pallas_call x1, Pallas kernels, per_device(): pl.pallas_call(norm_kernel, grid=(part // rows,), out_shape=(jax.ShapeDty...  5.85 us

profile of v4, /device:TPU:0, one launch (start us, length us, event | category | flops | bytes accessed | tf_op | source)
XLA Modules:
  0.0 75.2 jit_solution(13979746528856393169)
XLA Ops:
  0.6 68.7 %shard_map.112 = (bf16[128,4096]{1,0:T(8,128)(2,1)}, bf16[64,1024]{1,0:T(8,128)(2,1)}) custom-call(s32[8]{0:T(128)} %lens_s.1, s32[8]{0:T(128)} %accepted_s.1, s32[8,32]{1,0:T(8,128)} %parents_ref.1, bf16[256,1024]{1,0:T(8,128)(2,1)} %q_hbm.1, bf16[256,1024]{1,0:T(8,128)(2,1)} %fresh_hbm.1, bf16[8,4,256,1024]{3,2,1,0:T(8,128)(2,1)} %kv_hbm.1, ...), custom_call_target="tpu_custom_call" | custom-call | tf_op jit(solution)/shard_map/pallas_call | solution.py:405
  69.4 5.9 %shard_map.113 = (bf16[128,4096]{1,0:T(8,128)(2,1)}, bf16[128,4096]{1,0:T(8,128)(2,1)}, bf16[64,1024]{1,0:T(8,128)(2,1)}) custom-call(bf16[128,4096]{1,0:T(8,128)(2,1)} %get-tuple-element.8.hidden_ref, f32[1,4096]{1,0:T(1,128)} %bitcast.2, bf16[64,1024]{1,0:T(8,128)(2,1)} %get-tuple-element.9.path_ref), custom_call_target="tpu_custom_call" | custom-call | tf_op jit(solution)/shard_map/pallas_call | solution.py:451

commit v5 on v4

--- a/solution.py
+++ b/solution.py
@@ -59,7 +59,7 @@
     q_ref, fresh_ref, kv, w, residual, q_in, lens_own, lens_in, out_send, out_in, lse_send, lse_in,
     local_out, local_lse, tree, attention, proj_send, proj_in,
     load_sem, lens_send_sem, lens_recv_sem, q_send_sem, q_recv_sem, o_send_sem, o_recv_sem,
-    l_send_sem, l_recv_sem, p_send_sem, p_recv_sem,
+    l_send_sem, l_recv_sem, p_send_sem, p_recv_sem, f_send_sem,
 ):
     me, tp = lax.axis_index("req"), lax.axis_index("tp")
     tokens, width = q_ref.shape
@@ -147,12 +147,33 @@
     for p in range(1, pages):
         send_lens(p).start()
 
-    upfront = chunks // 2
-
-    @pl.loop(0, upfront)
+    odd = lax.rem(me, 2)
+    direct = (1 + 2 * odd, 2)
+
+    @pl.loop(0, chunks)
     def _(c):
-        for p in range(1, pages):
+        for p in direct:
             send_q(p, c).start()
+
+    def passed(c):
+        even_turn = 1 - lax.rem(c, 2)
+        return 2 * (1 - even_turn) + even_turn * (3 - 2 * odd)
+
+    def forward(c):
+        even_turn = 1 - lax.rem(c, 2)
+        source = passed(c)
+        target = even_turn * (1 + 2 * odd) + (1 - even_turn) * (3 - 2 * odd)
+        step = even_turn * (4 * odd - 2) + (1 - even_turn) * (1 - 2 * odd)
+        rows = pl.ds(first_row(c), chunk)
+        return pltpu.make_async_remote_copy(
+            q_in.at[source - 1, rows], q_in.at[target - 1, rows],
+            f_send_sem.at[c], q_recv_sem.at[target - 1, c],
+            device_id={"req": lax.rem(me + n_req + step, n_req)}, device_id_type=MESH,
+        )
+
+    def pass_on(c):
+        send_q(passed(c), c).wait_recv()
+        forward(c).start()
 
     marked = tree_masks(parents_ref[...], tokens)
     fold = indicator((iota((tokens, TREE), 0) & (TREE - 1)) == iota((tokens, TREE), 1))
@@ -292,6 +313,7 @@
             rows.append(jnp.zeros((LANES - chunk, LANES), F32))
             lse_send[p - 1, c] = jnp.concatenate(rows, axis=0).T[:8]
 
+    pass_on(0)
     first_loads[1].wait()
     loads[0].wait()
     local_chunk(first_row(0))
@@ -301,13 +323,12 @@
 
     @pl.loop(0, chunks)
     def _(c):
-        @pl.when(c < chunks - upfront)
+        @pl.when(c < chunks - 1)
         def _():
-            for p in range(1, pages):
-                send_q(p, c + upfront).start()
-
-        for p in range(1, pages):
-            send_q(p, c).wait_recv()
+            pass_on(c + 1)
+
+        for turn in range(1, pages - 1):
+            send_q(1 + lax.rem(passed(c) - 1 + turn, pages - 1), c).wait_recv()
         remote_chunk(first_row(c), c)
         for p in range(1, pages):
             send_lse(p, c).start()
@@ -372,8 +393,10 @@
 
     @pl.loop(0, chunks)
     def _(c):
+        forward(c).wait_send()
+        for p in direct:
+            send_q(p, c).wait_send()
         for p in range(1, pages):
-            send_q(p, c).wait_send()
             send_lse(p, c).wait_send()
             send_out(p, c).wait_send()
 
@@ -440,12 +463,13 @@
             dma((away, chunks)),
             dma((max(n_tp - 1, 1),)),
             dma((max(n_tp - 1, 1),)),
+            dma((chunks,)),
         ],
         compiler_params=pltpu.CompilerParams(
             collective_id=0, has_side_effects=True, vmem_limit_bytes=56 * 2**20
         ),
     )(cache_lens, accepted, parents, queries, new_kv, kv_pool, residual, w_out)
-    rows = 16
+    rows = min(part, 2 * TREE)
     row_block = pl.BlockSpec((rows, features), lambda i: (i, 0))
     whole_path = pl.BlockSpec(path.shape, lambda i: (0, 0))
     hidden_out, normed, path = pl.pallas_call(

time: 75.5 us -> 74.8 us (level)
  Pallas kernels: 74.6 us -> 73.7 us
    pallas_call x1, Pallas kernels: 5.85 us -> 2.58 us  [per_device(): pl.pallas_call(norm_kernel, grid=(part // rows,), out_shape=(jax.ShapeDty...]
    pallas_call x1, Pallas kernels: 68.7 us -> 71.2 us  [per_device(): pl.pallas_call(functools.partial(kernel, n_req, n_tp, chunk), out_shape=(...]
where the time goes in v5:
time: 74.8 us; the launch traced here: 74.4 us
  Pallas kernels  73.7 us (99%)
    pallas_call x1, Pallas kernels, per_device(): pl.pallas_call(functools.partial(kernel, n_req, n_tp, chunk), out_shape=(...  71.2 us
    pallas_call x1, Pallas kernels, per_device(): pl.pallas_call(norm_kernel, grid=(part // rows,), out_shape=(jax.ShapeDty...  2.58 us

profile of v5, /device:TPU:0, one launch (start us, length us, event | category | flops | bytes accessed | tf_op | source)
XLA Modules:
  0.0 74.4 jit_solution(6076677547608899373)
XLA Ops:
  0.6 71.2 %shard_map.112 = (bf16[128,4096]{1,0:T(8,128)(2,1)}, bf16[64,1024]{1,0:T(8,128)(2,1)}) custom-call(s32[8]{0:T(128)} %lens_s.1, s32[8]{0:T(128)} %accepted_s.1, s32[8,32]{1,0:T(8,128)} %parents_ref.1, bf16[256,1024]{1,0:T(8,128)(2,1)} %q_hbm.1, bf16[256,1024]{1,0:T(8,128)(2,1)} %fresh_hbm.1, bf16[8,4,256,1024]{3,2,1,0:T(8,128)(2,1)} %kv_hbm.1, ...), custom_call_target="tpu_custom_call" | custom-call | tf_op jit(solution)/shard_map/pallas_call | solution.py:428
  71.8 2.6 %shard_map.113 = (bf16[128,4096]{1,0:T(8,128)(2,1)}, bf16[128,4096]{1,0:T(8,128)(2,1)}, bf16[64,1024]{1,0:T(8,128)(2,1)}) custom-call(bf16[128,4096]{1,0:T(8,128)(2,1)} %get-tuple-element.8.hidden_ref, f32[1,4096]{1,0:T(1,128)} %bitcast.2, bf16[64,1024]{1,0:T(8,128)(2,1)} %get-tuple-element.9.path_ref), custom_call_target="tpu_custom_call" | custom-call | tf_op jit(solution)/shard_map/pallas_call | solution.py:475
